TPU v7x, 256 devices: a whole 4x4x8 slice. The times are simulated.
256 devices in a mesh: dp: 32 (over z, x), mp: 8 (over y, core).
Axes of the slice: x: 4, y: 4, z: 8, core: 2. Of those that a mesh axis runs over, the one named last changes fastest.
Arguments:
- tokens: bfloat16 [12288, 8192], P('dp', 'mp'), may hold values from -6 to 6
- frozen_base_weight: bfloat16 [8192, 8192], P('mp', 'dp'), may hold values from -0.0625 to 0.0625
- tenant_down_factors: bfloat16 [64, 8192, 64], P('dp', 'mp'), may hold values from -0.0625 to 0.0625
- tenant_up_factors: bfloat16 [64, 8192, 64], P('dp', 'mp'), may hold values from -0.75 to 0.75
- cotangent: bfloat16 [12288, 8192], P('dp', 'mp'), may hold values from -6 to 6
- block_tenant_index: int32 [96], replicated, may hold values from 0 to 63
- ranks: int32 [64], replicated, may hold values from 8 to 64
Outputs:
- layer_out: bfloat16 [12288, 8192], P('dp', 'mp')
- input_grad: bfloat16 [12288, 8192], P('dp', 'mp')
- down_grad: float32 [64, 8192, 64], P('dp', 'mp')
- up_grad: float32 [64, 8192, 64], P('dp', 'mp')
Inputs may be any that keep to these rules, and one draw needn't show every extreme that they name: `block_tenant_index`: tenant of each block of 128 consecutive rows; some tenants own many blocks, some none. `ranks`: rank columns at or past a tenant's rank are unused.
All inputs are finite; a program needn't handle non-finite values.
Results may differ from a plain program's by a relative error of at most 0.017.
Values may be sent and summed in bfloat16 or wider, within the bound.
A program may use at most 128 MiB of HBM per device.

v0:
```python
import jax
import jax.numpy as jnp
from jax import lax
from jax.sharding import PartitionSpec as P

BLOCK = 128


def local(
    tokens,
    frozen_base_weight,
    tenant_down_factors,
    tenant_up_factors,
    cotangent,
    block_tenant_index,
    ranks,
):
    num_peers = lax.axis_size("dp")
    my_index = lax.axis_index("dp")
    row_count, feat_width = tokens.shape
    block_count = row_count // BLOCK
    held_tenant_count = tenant_down_factors.shape[0]
    rank_padding = tenant_down_factors.shape[2]
    count_of_tenants = held_tenant_count * num_peers
    piece_width = feat_width // num_peers
    block_total = block_count * num_peers
    rank_positions = jnp.arange(rank_padding, dtype=jnp.int32)
    kept_ranks = (rank_positions[None, :] < ranks[:, None]).astype(jnp.float32)
    coef_table = kept_ranks * (16.0 / ranks.astype(jnp.float32))[:, None]
    tenant_range = jnp.arange(count_of_tenants, dtype=jnp.int32)
    my_tenants = lax.dynamic_slice_in_dim(block_tenant_index, my_index * block_count, block_count)
    select_onehot = (my_tenants[:, None] == tenant_range[None, :]).astype(jnp.float32)
    block_coef = jnp.dot(select_onehot, coef_table, precision=lax.Precision.HIGHEST)
    stacked_factors = jnp.concatenate([tenant_down_factors, tenant_up_factors], axis=2)
    split_factors = stacked_factors.reshape(
        held_tenant_count, num_peers, piece_width, 2 * rank_padding
    )
    received = lax.all_to_all(split_factors, "dp", split_axis=1, concat_axis=0, tiled=True)
    piece_table = received.reshape(count_of_tenants, piece_width * 2 * rank_padding)
    selection = block_tenant_index.reshape(num_peers, block_count)
    outgoing = piece_table[selection].reshape(num_peers, block_count, piece_width, 2 * rank_padding)
    arrived = lax.all_to_all(outgoing, "dp", split_axis=0, concat_axis=2, tiled=True)
    factors = arrived.reshape(block_count, feat_width, 2 * rank_padding)
    down_factor = factors[:, :, :rank_padding]
    up_factor = factors[:, :, rank_padding:]
    tok_blocks = tokens.reshape(block_count, BLOCK, feat_width)
    low_partial = jnp.einsum(
        "bid,bdr->bir", tok_blocks, down_factor, preferred_element_type=jnp.float32
    )
    pre_low = lax.psum(low_partial.astype(jnp.bfloat16), "mp").astype(jnp.float32)
    low_rank = (pre_low * block_coef[:, None, :]).astype(jnp.bfloat16)
    weights_all = lax.all_gather(frozen_base_weight, "dp", axis=1, tiled=True)
    base_terms = jnp.dot(tokens, weights_all, preferred_element_type=jnp.float32)
    base_share = lax.psum_scatter(
        base_terms.astype(jnp.bfloat16), "mp", scatter_dimension=1, tiled=True
    ).astype(jnp.float32)
    adapter_out = jnp.einsum(
        "bir,ber->bie", low_rank, up_factor, preferred_element_type=jnp.float32
    )
    layer_out = (base_share + adapter_out.reshape(row_count, feat_width)).astype(jnp.bfloat16)
    cot_blocks = cotangent.reshape(block_count, BLOCK, feat_width)
    dlow_partial = jnp.einsum(
        "bie,ber->bir", cot_blocks, up_factor, preferred_element_type=jnp.float32
    )
    pre_dlow = lax.psum(dlow_partial.astype(jnp.bfloat16), "mp").astype(jnp.float32)
    dlow_rank = (pre_dlow * block_coef[:, None, :]).astype(jnp.bfloat16)
    full_cotangent = lax.all_gather(cotangent, "mp", axis=1, tiled=True)
    base_grad = lax.dot_general(
        full_cotangent, weights_all, (((1,), (1,)), ((), ())), preferred_element_type=jnp.float32
    )
    adapter_grad = jnp.einsum(
        "bir,bdr->bid", dlow_rank, down_factor, preferred_element_type=jnp.float32
    )
    input_grad = (base_grad + adapter_grad.reshape(row_count, feat_width)).astype(jnp.bfloat16)
    block_down = jnp.einsum(
        "bid,bir->bdr", tok_blocks, dlow_rank, preferred_element_type=jnp.float32
    )
    block_up = jnp.einsum("bie,bir->ber", cot_blocks, low_rank, preferred_element_type=jnp.float32)
    block_grads = jnp.concatenate([block_down, block_up], axis=2)
    split_grads = block_grads.reshape(block_count, num_peers, piece_width, 2 * rank_padding)
    grad_arrived = lax.all_to_all(
        split_grads.astype(jnp.bfloat16), "dp", split_axis=1, concat_axis=0, tiled=True
    ).astype(split_grads.dtype)
    grad_rows = grad_arrived.reshape(block_total, piece_width * 2 * rank_padding)
    tenant_onehot = (block_tenant_index[None, :] == tenant_range[:, None]).astype(jnp.float32)
    tenant_sums = jnp.dot(tenant_onehot, grad_rows, precision=lax.Precision.HIGHEST)
    owner_bound = tenant_sums.reshape(num_peers, held_tenant_count, piece_width, 2 * rank_padding)
    owned_grads = lax.all_to_all(
        owner_bound.astype(jnp.bfloat16), "dp", split_axis=0, concat_axis=2, tiled=True
    ).astype(owner_bound.dtype)
    owned_grads = owned_grads.reshape(held_tenant_count, feat_width, 2 * rank_padding)
    down_grad = owned_grads[:, :, :rank_padding]
    up_grad = owned_grads[:, :, rank_padding:]
    return (layer_out, input_grad, down_grad, up_grad)


def solution(mesh):
    return jax.shard_map(
        local,
        mesh=mesh,
        in_specs=(
            P("dp", "mp"),
            P("mp", "dp"),
            P("dp", "mp", None),
            P("dp", "mp", None),
            P("dp", "mp"),
            P(),
            P(),
        ),
        out_specs=(P("dp", "mp"), P("dp", "mp"), P("dp", "mp", None), P("dp", "mp", None)),
        check_vma=False,
    )
```

profile of v0, /device:TPU:8, one launch (start us, length us, event | category | flops | bytes accessed | tf_op | source)
XLA Modules:
  0.0 286.6 jit_solution(3312873384921859337)
XLA Ops:
  8.7 1.2 copy.26
  10.0 1.2 copy.25
  12.4 11.3 %all-to-all-start = ((bf16[2,32,32,128]{3,2,0,1:T(8,128)(2,1)}), bf16[2,32,32,128]{3,2,0,1:T(8,128)(2,1)S(1)}, u32[]{:S(2)}, u32[]{:S(2)}) async-start(bf16[2,32,32,128]{3,2,0,1:T(8,128)(2,1)} %copy.27), calls=%async_computation.1 | async-start | bytes 1048576 | tf_op jit(solution)/shard_map/all_to_all | solution.py:38
  24.6 20.3 %all-to-all-done = bf16[2,32,32,128]{3,2,0,1:T(8,128)(2,1)S(1)} async-done(((bf16[2,32,32,128]{3,2,0,1:T(8,128)(2,1)}), bf16[2,32,32,128]{3,2,0,1:T(8,128)(2,1)S(1)}, u32[]{:S(2)}, u32[]{:S(2)}) %all-to-all-start) | async-done | bytes 524320 | tf_op jit(solution)/shard_map/all_to_all | solution.py:38
  45.1 1.0 gather_fusion
  46.3 30.9 %all_to_all.54 = bf16[32,3,32,128]{3,2,1,0:T(8,128)(2,1)S(1)} all-to-all(bf16[32,3,32,128]{3,2,1,0:T(8,128)(2,1)S(1)} %bitcast.90), channel_id=1, replica_groups=mesh['dp'=32,'mp'=8] {'dp'}, dimensions={0} | all-to-all | bytes 1572864 | tf_op jit(solution)/shard_map/all_to_all | solution.py:42
  77.3 1.1 fusion.4
  78.3 1.4 fusion.5
  80.6 103.5 %all-gather.3.cloned.1.call-done = bf16[1024,8192]{1,0:T(8,128)(2,1)} async-done(((bf16[1024,256]{1,0:T(8,128)(2,1)}), bf16[1024,8192]{1,0:T(8,128)(2,1)}) %all-gather.3.cloned.1.call-update) | async-done | bytes 16777232 | tf_op jit(solution)/shard_map/all_gather | solution.py:52
  184.1 14.3 %convolution_convert_fusion = bf16[384,8192]{1,0:T(8,128)(2,1)} fusion(bf16[384,1024]{1,0:T(8,128)(2,1)S(1)} %copy-done, bf16[1024,8192]{1,0:T(8,128)(2,1)} %all-gather.3.cloned.1.call-done), kind=kOutput, calls=%fused_computation.1 | convolution fusion | flops 6445596672 | bytes 23855104 | tf_op jit(solution)/shard_map/dot_general | solution.py:53
  199.6 1.1 fusion.3
  200.7 1.1 fusion.2
  203.2 5.5 %all-to-all-start.2 = ((bf16[3,32,32,128]{3,2,0,1:T(8,128)(2,1)}), bf16[3,32,32,128]{3,2,0,1:T(8,128)(2,1)S(1)}, u32[]{:S(2)}, u32[]{:S(2)}) async-start(bf16[3,32,32,128]{3,2,0,1:T(8,128)(2,1)} %copy.32), calls=%async_computation.3 | async-start | bytes 1572864 | tf_op jit(solution)/shard_map/all_to_all | solution.py:81
  208.8 20.0 %all-to-all-done.2 = bf16[3,32,32,128]{3,2,0,1:T(8,128)(2,1)S(1)} async-done(((bf16[3,32,32,128]{3,2,0,1:T(8,128)(2,1)}), bf16[3,32,32,128]{3,2,0,1:T(8,128)(2,1)S(1)}, u32[]{:S(2)}, u32[]{:S(2)}) %all-to-all-start.2) | async-done | bytes 786464 | tf_op jit(solution)/shard_map/all_to_all | solution.py:81
  229.2 1.0 copy.34
  230.2 5.3 %all-to-all-start.3 = ((bf16[32,2,32,128]{3,2,1,0:T(8,128)(2,1)}), bf16[32,2,32,128]{3,2,1,0:T(8,128)(2,1)}, u32[]{:S(2)}, u32[]{:S(2)}) async-start(bf16[32,2,32,128]{3,2,1,0:T(8,128)(2,1)} %copy.34), calls=%async_computation.4 | async-start | bytes 1048576 | tf_op jit(solution)/shard_map/all_to_all | solution.py:88
  236.2 1.7 fusion.11
  237.9 12.4 %all-to-all-done.3 = bf16[32,2,32,128]{3,2,1,0:T(8,128)(2,1)} async-done(((bf16[32,2,32,128]{3,2,1,0:T(8,128)(2,1)}), bf16[32,2,32,128]{3,2,1,0:T(8,128)(2,1)}, u32[]{:S(2)}, u32[]{:S(2)}) %all-to-all-start.3) | async-done | bytes 524320 | tf_op jit(solution)/shard_map/all_to_all | solution.py:88
  250.3 1.2 bitcast_convert_fusion
  251.5 1.6 fusion.24
  253.1 2.3 copy.36
  255.5 2.3 copy.37
  257.8 19.0 %fusion = bf16[384,1024]{1,0:T(8,128)(2,1)} fusion(f32[3,128,1024]{2,1,0:T(8,128)} %fusion.11, bf16[384,8192]{1,0:T(8,128)(2,1)} %all-gather.5.cloned.1.call-done, bf16[1024,8192]{1,0:T(8,128)(2,1)} %all-gather.3.cloned.1.call-done), kind=kOutput, calls=%fused_computation.3 | convolution fusion | flops 6443237376 | bytes 25427968 | tf_op jit(solution)/shard_map/dot_general | solution.py:68
  276.8 2.4 fusion.1
  (43 shorter events, 7.6 us)
Async XLA Ops:
  8.0 69.3 %copy-start = (bf16[384,1024]{1,0:T(8,128)(2,1)S(1)}, bf16[384,1024]{1,0:T(8,128)(2,1)}, u32[]{:S(2)}) copy-start(bf16[384,1024]{1,0:T(8,128)(2,1)} %param.7) | copy-start | bytes 2359300
  8.0 176.1 %all-gather.3.cloned.1.call-start = ((), (), s32[]{:S(2)}) async-start(), calls=%async_computation.5 | async-start | bytes 17301504 | tf_op jit(solution)/shard_map/all_gather | solution.py:52
  12.4 32.5 %all-to-all-start = ((bf16[2,32,32,128]{3,2,0,1:T(8,128)(2,1)}), bf16[2,32,32,128]{3,2,0,1:T(8,128)(2,1)S(1)}, u32[]{:S(2)}, u32[]{:S(2)}) async-start(bf16[2,32,32,128]{3,2,0,1:T(8,128)(2,1)} %copy.27), calls=%async_computation.1 | async-start | bytes 1048576 | tf_op jit(solution)/shard_map/all_to_all | solution.py:38
  23.7 175.7 %all-reduce.3.cloned.1.call-start = ((), (), s32[]{:S(2)}) async-start(), calls=%async_computation.8 | async-start | bytes 196608 | tf_op jit(solution)/shard_map/psum | solution.py:50
  45.1 33.2 %copy-start.1 = (bf16[384,1024]{1,0:T(8,128)(2,1)S(1)}, bf16[384,1024]{1,0:T(8,128)(2,1)}, u32[]{:S(2)}) copy-start(bf16[384,1024]{1,0:T(8,128)(2,1)} %param.11) | copy-start | bytes 2359300
  79.8 178.0 %all-gather.5.cloned.1.call-start = ((), (), s32[]{:S(2)}) async-start(), calls=%async_computation.7 | async-start | bytes 7077888 | tf_op jit(solution)/shard_map/all_gather | solution.py:67
  80.6 196.3 %reduce-scatter.2.cloned.1.call-start = ((), (), s32[]{:S(2)}) async-start(), calls=%async_computation.6 | async-start | bytes 7077888 | tf_op jit(solution)/shard_map/reduce_scatter | solution.py:54
  198.4 0.7 copy-start.5
  198.4 0.7 copy-start.6
  198.4 1.2 copy-start.2
  199.4 36.1 %copy-start.4 = (bf16[3,128,64]{1,2,0:T(8,128)(2,1)S(1)}, bf16[3,128,64]{1,2,0:T(8,128)(2,1)}, u32[]{:S(2)}) copy-start(bf16[3,128,64]{1,2,0:T(8,128)(2,1)} %get-tuple-element.12) | copy-start | bytes 147460
  201.8 34.4 %copy-start.3 = (bf16[3,128,64]{1,2,0:T(8,128)(2,1)S(1)}, bf16[3,128,64]{1,2,0:T(8,128)(2,1)}, u32[]{:S(2)}) copy-start(bf16[3,128,64]{1,2,0:T(8,128)(2,1)} %get-tuple-element.13) | copy-start | bytes 147460
  203.2 25.6 %all-to-all-start.2 = ((bf16[3,32,32,128]{3,2,0,1:T(8,128)(2,1)}), bf16[3,32,32,128]{3,2,0,1:T(8,128)(2,1)S(1)}, u32[]{:S(2)}, u32[]{:S(2)}) async-start(bf16[3,32,32,128]{3,2,0,1:T(8,128)(2,1)} %copy.32), calls=%async_computation.3 | async-start | bytes 1572864 | tf_op jit(solution)/shard_map/all_to_all | solution.py:81
  230.2 20.2 %all-to-all-start.3 = ((bf16[32,2,32,128]{3,2,1,0:T(8,128)(2,1)}), bf16[32,2,32,128]{3,2,1,0:T(8,128)(2,1)}, u32[]{:S(2)}, u32[]{:S(2)}) async-start(bf16[32,2,32,128]{3,2,1,0:T(8,128)(2,1)} %copy.34), calls=%async_computation.4 | async-start | bytes 1048576 | tf_op jit(solution)/shard_map/all_to_all | solution.py:88
Sparse Core Ops, SparseCore 0:
  11.6 172.4 all-gather.2
  186.1 47.7 all-gather.4
Sparse Core Ops, SparseCore 1:
  79.9 59.3 all-reduce.2
  198.5 54.7 reduce-scatter.1
where the time goes:
time: 287 us
  waiting for transfers between devices  158 us (55%)
  matrix products  41.1 us (14%)
  blocking collectives  30.9 us (11%)
  starting transfers between devices  22.3 us (8%)
  between operations  15.7 us (5%)
  local copies, waits for them, and re-layouts  15.2 us (5%)
  other arithmetic  3.91 us (1%)
    all_gather x1, waiting for transfers between devices, local(): weights_all = lax.all_gather(frozen_base_weight, 'dp', axis=1, tiled=True)  103 us
    all_to_all x1, blocking collectives, local(): lax.all_to_all(outgoing, 'dp', split_axis=0, concat_axis=2, tiled=True)  30.9 us
    all_to_all x1, waiting for transfers between devices, local(): lax.all_to_all(split_factors, 'dp', split_axis=1, concat_axis=0, tiled=True)  20.3 us
    all_to_all x1, waiting for transfers between devices, local(): lax.all_to_all(split_grads.astype(jnp.bfloat16), 'dp', split_axis=1, conc...  20 us
    dot_general x1, matrix products, local(): lax.dot_general(full_cotangent, weights_all, (((1,), (1,)), ((), ())), pr...  19 us
    dot_general x1, matrix products, local(): jnp.dot(tokens, weights_all, preferred_element_type=jnp.float32)  14.3 us
    all_to_all x1, waiting for transfers between devices, local(): lax.all_to_all(owner_bound.astype(jnp.bfloat16), 'dp', split_axis=0, conc...  12.4 us
    all_to_all x1, starting transfers between devices, local(): lax.all_to_all(split_factors, 'dp', split_axis=1, concat_axis=0, tiled=True)  11.3 us
  transfers between devices with their start and end apart: 7, of which 4 were waited for; matrix products, arithmetic and copies ran while one was open for 20% of the time, Pallas kernels for 0%

commit v1 on v0

--- a/solution.py
+++ b/solution.py
@@ -4,6 +4,13 @@
 from jax.sharding import PartitionSpec as P
 
 BLOCK = 128
+
+
+def swapped_in(x, axis, dim):
+    size = lax.axis_size(axis)
+    pieces = jnp.stack([x for _ in range(size)])
+    pieces = lax.all_to_all(pieces, axis, split_axis=0, concat_axis=0)
+    return jnp.concatenate(pieces, axis=dim)
 
 
 def local(
@@ -49,7 +56,7 @@
     )
     pre_low = lax.psum(low_partial.astype(jnp.bfloat16), "mp").astype(jnp.float32)
     low_rank = (pre_low * block_coef[:, None, :]).astype(jnp.bfloat16)
-    weights_all = lax.all_gather(frozen_base_weight, "dp", axis=1, tiled=True)
+    weights_all = swapped_in(frozen_base_weight, "dp", 1)
     base_terms = jnp.dot(tokens, weights_all, preferred_element_type=jnp.float32)
     base_share = lax.psum_scatter(
         base_terms.astype(jnp.bfloat16), "mp", scatter_dimension=1, tiled=True

time: 287 us -> 578 us (2.01)
  waiting for transfers between devices: 158 us -> 457 us
  blocking collectives: 30.9 us -> 0 us
  starting transfers between devices: 22.3 us -> 45.1 us
  local copies, waits for them, and re-layouts: 15.2 us -> 23.4 us
  matrix products: 41.1 us -> 34.3 us
    all_to_all x0 -> x2, waiting for transfers between devices: none -> 405 us  [the longest x1 384 us: swapped_in(): pieces = lax.all_to_all(pieces, axis, split_axis=0, concat_axis=0)]
    all_gather x1 -> x0, waiting for transfers between devices: 103 us -> none  [local(): weights_all = lax.all_gather(frozen_base_weight, 'dp', axis=1, tiled=True)]
    all_to_all x1 -> x0, blocking collectives: 30.9 us -> none  [local(): lax.all_to_all(outgoing, 'dp', split_axis=0, concat_axis=2, tiled=True)]
    all_to_all x1, starting transfers between devices: 5.54 us -> 18.4 us  [local(): lax.all_to_all(split_grads.astype(jnp.bfloat16), 'dp', split_axis=1, conc...]
    all_to_all x0 -> x2, starting transfers between devices: none -> 10.2 us  [the longest x1 5.55 us: swapped_in(): pieces = lax.all_to_all(pieces, axis, split_axis=0, concat_axis=0)]
    another operation x0 -> x1, local copies, waits for them, and re-layouts: none -> 5.96 us  [swapped_in(): pieces = jnp.stack([x for _ in range(size)])]
  transfers between devices with their start and end apart: 7 -> 8, of which waited for: 4 -> 5; matrix products, arithmetic and copies ran while one was open for 20% -> 8% of each run, Pallas kernels for 0% -> 0%
where the time goes in v1:
time: 578 us; the launch traced here: 577 us
  waiting for transfers between devices  457 us (79%)
  starting transfers between devices  45.1 us (8%)
  matrix products  34.3 us (6%)
  local copies, waits for them, and re-layouts  23.4 us (4%)
  between operations  14 us (2%)
    all_to_all x1, waiting for transfers between devices, swapped_in(): pieces = lax.all_to_all(pieces, axis, split_axis=0, concat_axis=0)  384 us
    all_to_all x1, waiting for transfers between devices, local(): lax.all_to_all(split_grads.astype(jnp.bfloat16), 'dp', split_axis=1, conc...  21.3 us
    all_to_all x1, waiting for transfers between devices, local(): lax.all_to_all(outgoing, 'dp', split_axis=0, concat_axis=2, tiled=True)  20.6 us
    all_to_all x1, starting transfers between devices, local(): lax.all_to_all(split_grads.astype(jnp.bfloat16), 'dp', split_axis=1, conc...  18.4 us
    all_to_all x1, waiting for transfers between devices, local(): lax.all_to_all(split_factors, 'dp', split_axis=1, concat_axis=0, tiled=True)  16.8 us
    dot_general x1, matrix products, local(): lax.dot_general(full_cotangent, weights_all, (((1,), (1,)), ((), ())), pr...  14.6 us
    all_to_all x1, waiting for transfers between devices, local(): lax.all_to_all(owner_bound.astype(jnp.bfloat16), 'dp', split_axis=0, conc...  13.2 us
    dot_general x1, matrix products, local(): jnp.dot(tokens, weights_all, preferred_element_type=jnp.float32)  12 us
  transfers between devices with their start and end apart: 8, of which 5 were waited for; matrix products, arithmetic and copies ran while one was open for 8% of the time, Pallas kernels for 0%

profile of v1, /device:TPU:8, one launch (start us, length us, event | category | flops | bytes accessed | tf_op | source)
XLA Modules:
  0.0 577.5 jit_solution(15548561368634487102)
XLA Ops:
  7.2 1.3 copy.28
  8.5 1.2 copy.27
  10.9 11.3 %all-to-all-start.1 = ((bf16[2,32,32,128]{3,2,0,1:T(8,128)(2,1)}), bf16[2,32,32,128]{3,2,0,1:T(8,128)(2,1)S(1)}, u32[]{:S(2)}, u32[]{:S(2)}) async-start(bf16[2,32,32,128]{3,2,0,1:T(8,128)(2,1)} %copy.29), calls=%async_computation.2 | async-start | bytes 1048576 | tf_op jit(solution)/shard_map/all_to_all | solution.py:45
  23.1 16.8 %all-to-all-done.1 = bf16[2,32,32,128]{3,2,0,1:T(8,128)(2,1)S(1)} async-done(((bf16[2,32,32,128]{3,2,0,1:T(8,128)(2,1)}), bf16[2,32,32,128]{3,2,0,1:T(8,128)(2,1)S(1)}, u32[]{:S(2)}, u32[]{:S(2)}) %all-to-all-start.1) | async-done | bytes 524320 | tf_op jit(solution)/shard_map/all_to_all | solution.py:45
  42.2 4.7 all-to-all-start.2
  46.9 1.2 copy.26
  48.1 20.6 %all-to-all-done.2 = bf16[32,3,32,128]{3,2,1,0:T(8,128)(2,1)S(1)} async-done(((bf16[32,3,32,128]{3,2,1,0:T(8,128)(2,1)}), bf16[32,3,32,128]{3,2,1,0:T(8,128)(2,1)S(1)}, u32[]{:S(2)}, u32[]{:S(2)}) %all-to-all-start.2) | async-done | bytes 786464 | tf_op jit(solution)/shard_map/all_to_all | solution.py:49
  68.7 6.0 %stack.2 = bf16[32,1024,256]{1,2,0:T(8,128)(2,1)} broadcast(bf16[1024,256]{0,1:T(8,128)(2,1)S(1)} %copy.26), dimensions={1,2} | broadcast | bytes 17301504 | tf_op jit(solution)/shard_map/stack | solution.py:11
  74.7 5.5 all-to-all-start
  81.4 1.4 fusion.5
  83.7 384.2 %all-to-all-done = bf16[32,1024,256]{1,2,0:T(8,128)(2,1)} async-done(((bf16[32,1024,256]{1,2,0:T(8,128)(2,1)}), bf16[32,1024,256]{1,2,0:T(8,128)(2,1)}, u32[]{:S(2)}, u32[]{:S(2)}) %all-to-all-start) | async-done | bytes 16777248 | tf_op jit(solution)/shard_map/all_to_all | solution.py:12
  467.9 12.0 %convolution_convert_fusion = bf16[384,8192]{1,0:T(8,128)(2,1)} fusion(bf16[384,1024]{1,0:T(8,128)(2,1)S(1)} %copy-done, bf16[1024,8192]{0,1:T(8,128)(2,1)} %bitcast.1), kind=kOutput, calls=%fused_computation.1 | convolution fusion | flops 6445596672 | bytes 23855104 | tf_op jit(solution)/shard_map/dot_general | solution.py:60
  482.2 1.1 fusion.2
  484.7 18.4 %all-to-all-start.3 = ((bf16[3,32,32,128]{3,2,0,1:T(8,128)(2,1)}), bf16[3,32,32,128]{3,2,0,1:T(8,128)(2,1)S(1)}, u32[]{:S(2)}, u32[]{:S(2)}) async-start(bf16[3,32,32,128]{3,2,0,1:T(8,128)(2,1)} %copy.34), calls=%async_computation.4 | async-start | bytes 1572864 | tf_op jit(solution)/shard_map/all_to_all | solution.py:88
  503.1 21.3 %all-to-all-done.3 = bf16[3,32,32,128]{3,2,0,1:T(8,128)(2,1)S(1)} async-done(((bf16[3,32,32,128]{3,2,0,1:T(8,128)(2,1)}), bf16[3,32,32,128]{3,2,0,1:T(8,128)(2,1)S(1)}, u32[]{:S(2)}, u32[]{:S(2)}) %all-to-all-start.3) | async-done | bytes 786464 | tf_op jit(solution)/shard_map/all_to_all | solution.py:88
  525.8 5.1 all-to-all-start.4
  531.6 1.7 fusion.11
  533.2 13.2 %all-to-all-done.4 = bf16[32,2,32,128]{3,2,1,0:T(8,128)(2,1)} async-done(((bf16[32,2,32,128]{3,2,1,0:T(8,128)(2,1)}), bf16[32,2,32,128]{3,2,1,0:T(8,128)(2,1)}, u32[]{:S(2)}, u32[]{:S(2)}) %all-to-all-start.4) | async-done | bytes 524320 | tf_op jit(solution)/shard_map/all_to_all | solution.py:95
  546.4 1.2 bitcast_convert_fusion
  547.6 1.7 fusion.24
  549.3 2.3 copy.38
  551.6 2.3 copy.39
  554.0 14.6 %fusion = bf16[384,1024]{1,0:T(8,128)(2,1)} fusion(f32[3,128,1024]{2,1,0:T(8,128)} %fusion.11, bf16[384,8192]{1,0:T(8,128)(2,1)} %all-gather.2.cloned.1.call-done, bf16[1024,8192]{0,1:T(8,128)(2,1)} %bitcast.1), kind=kOutput, calls=%fused_computation.3 | convolution fusion | flops 6443237376 | bytes 25427968 | tf_op jit(solution)/shard_map/dot_general | solution.py:75
  568.6 2.4 fusion.1
  (47 shorter events, 12.0 us)
Async XLA Ops:
  7.2 73.2 %copy-start = (bf16[384,1024]{1,0:T(8,128)(2,1)S(1)}, bf16[384,1024]{1,0:T(8,128)(2,1)}, u32[]{:S(2)}) copy-start(bf16[384,1024]{1,0:T(8,128)(2,1)} %param.7) | copy-start | bytes 2359300
  10.9 29.0 %all-to-all-start.1 = ((bf16[2,32,32,128]{3,2,0,1:T(8,128)(2,1)}), bf16[2,32,32,128]{3,2,0,1:T(8,128)(2,1)S(1)}, u32[]{:S(2)}, u32[]{:S(2)}) async-start(bf16[2,32,32,128]{3,2,0,1:T(8,128)(2,1)} %copy.29), calls=%async_computation.2 | async-start | bytes 1048576 | tf_op jit(solution)/shard_map/all_to_all | solution.py:45
  42.2 26.5 %all-to-all-start.2 = ((bf16[32,3,32,128]{3,2,1,0:T(8,128)(2,1)}), bf16[32,3,32,128]{3,2,1,0:T(8,128)(2,1)S(1)}, u32[]{:S(2)}, u32[]{:S(2)}) async-start(bf16[32,3,32,128]{3,2,1,0:T(8,128)(2,1)} %bitcast.43), calls=%async_computation.3 | async-start | bytes 1572864 | tf_op jit(solution)/shard_map/all_to_all | solution.py:49
  74.7 6.8 %copy-start.2 = (bf16[384,1024]{1,0:T(8,128)(2,1)S(1)}, bf16[384,1024]{1,0:T(8,128)(2,1)}, u32[]{:S(2)}) copy-start(bf16[384,1024]{1,0:T(8,128)(2,1)} %param.11) | copy-start | bytes 2359300
  74.7 393.3 %all-to-all-start = ((bf16[32,1024,256]{1,2,0:T(8,128)(2,1)}), bf16[32,1024,256]{1,2,0:T(8,128)(2,1)}, u32[]{:S(2)}, u32[]{:S(2)}) async-start(bf16[32,1024,256]{1,2,0:T(8,128)(2,1)} %stack.2), calls=%async_computation | async-start | bytes 33554432 | tf_op jit(solution)/shard_map/all_to_all | solution.py:12
  80.2 400.7 %all-reduce.3.cloned.1.call-start = ((), (), s32[]{:S(2)}) async-start(), calls=%async_computation.8 | async-start | bytes 196608 | tf_op jit(solution)/shard_map/psum | solution.py:57
  82.9 471.1 %all-gather.2.cloned.1.call-start = ((), (), s32[]{:S(2)}) async-start(), calls=%async_computation.7 | async-start | bytes 7077888 | tf_op jit(solution)/shard_map/all_gather | solution.py:74
  83.6 485.0 %reduce-scatter.2.cloned.1.call-start = ((), (), s32[]{:S(2)}) async-start(), calls=%async_computation.6 | async-start | bytes 7077888 | tf_op jit(solution)/shard_map/reduce_scatter | solution.py:61
  479.9 0.7 copy-start.6
  479.9 0.7 copy-start.7
  479.9 1.2 copy-start.3
  480.9 50.0 %copy-start.5 = (bf16[3,128,64]{1,2,0:T(8,128)(2,1)S(1)}, bf16[3,128,64]{1,2,0:T(8,128)(2,1)}, u32[]{:S(2)}) copy-start(bf16[3,128,64]{1,2,0:T(8,128)(2,1)} %get-tuple-element.12) | copy-start | bytes 147460
  483.3 48.2 %copy-start.4 = (bf16[3,128,64]{1,2,0:T(8,128)(2,1)S(1)}, bf16[3,128,64]{1,2,0:T(8,128)(2,1)}, u32[]{:S(2)}) copy-start(bf16[3,128,64]{1,2,0:T(8,128)(2,1)} %get-tuple-element.13) | copy-start | bytes 147460
  484.7 39.7 %all-to-all-start.3 = ((bf16[3,32,32,128]{3,2,0,1:T(8,128)(2,1)}), bf16[3,32,32,128]{3,2,0,1:T(8,128)(2,1)S(1)}, u32[]{:S(2)}, u32[]{:S(2)}) async-start(bf16[3,32,32,128]{3,2,0,1:T(8,128)(2,1)} %copy.34), calls=%async_computation.4 | async-start | bytes 1572864 | tf_op jit(solution)/shard_map/all_to_all | solution.py:88
  525.8 20.6 %all-to-all-start.4 = ((bf16[32,2,32,128]{3,2,1,0:T(8,128)(2,1)}), bf16[32,2,32,128]{3,2,1,0:T(8,128)(2,1)}, u32[]{:S(2)}, u32[]{:S(2)}) async-start(bf16[32,2,32,128]{3,2,1,0:T(8,128)(2,1)} %copy.36), calls=%async_computation.5 | async-start | bytes 1048576 | tf_op jit(solution)/shard_map/all_to_all | solution.py:95
  554.0 17.0 %copy-start.1 = (bf16[384,1024]{1,0:T(8,128)(2,1)S(1)}, bf16[384,1024]{1,0:T(8,128)(2,1)}, u32[]{:S(2)}) copy-start(bf16[384,1024]{1,0:T(8,128)(2,1)} %param.7) | copy-start | bytes 2359300
Sparse Core Ops, SparseCore 0:
  84.1 63.0 all-reduce.2
  149.2 44.2 all-gather.1
  480.1 52.9 reduce-scatter.1
